TPU v7x, 32 devices: a whole 2x2x4 slice. The times are simulated.
32 devices in a mesh: sky: 8 (over y, x, core), gz: 4 (over z).
Axes of the slice: x: 2, y: 2, z: 4, core: 2. Of those that a mesh axis runs over, the one named last changes fastest.
Arguments:
- spectra: bfloat16 [2048, 1032], P('sky', 'gz'), may hold values from -6 to 6
- kernel: bfloat16 [2048, 16], P('sky'), may hold values from 0.049804688 to 0.59765625
- owner: int32 [2048, 1], P('sky'), may hold values from 0 to 7; in each aligned block of 256 rows (0 to 255, 256 to 511, ...) at most 40 rows name the same one
- offset: int32 [2048], P('sky'), may hold values from 0 to 8191
Outputs:
- spectrum: float32 [2, 256, 256, 1032], P(None, None, ('sky', 'gz'))
Inputs may be any that keep to these rules, and one draw needn't show every extreme that they name: `owner`: in each aligned block of 256 rows no sky index is named by more than 40 rows, a bound that some block reaches.
All inputs are finite; a program needn't handle non-finite values.
Results may differ from a plain program's by a relative error of at most 0.0063.
Values may be sent and summed in bfloat16 or wider, within the bound.
A program may use at most 128 MiB of HBM per device.

v0:
```python
import math

import jax
import jax.numpy as jnp
import numpy as np
from jax import lax
from jax.sharding import PartitionSpec as P

NX = 256
NY = 256
NW = 1032
KSIDE = 4
BF = jnp.bfloat16
F32 = jnp.float32


def dft_tables(length):
    steps = np.arange(length)
    angles = (steps[:, None] * steps[None, :] % length).astype(np.float64) * (2.0 * math.pi / length)
    factor = 1.0 / math.sqrt(length)
    return np.cos(angles) * factor, np.sin(angles) * factor


def pack(spectra, kernel, owner, offset):
    sky_count, gz_count = lax.axis_size("sky"), lax.axis_size("gz")
    fibre_count, slab = spectra.shape
    cap = fibre_count * 5 // (4 * sky_count)
    slots = sky_count * cap
    own = owner[:, 0]
    order = jnp.arange(fibre_count, dtype=jnp.int32)
    earlier = (own[None, :] == own[:, None]) & (order[None, :] < order[:, None])
    position = own * cap + jnp.sum(earlier.astype(jnp.int32), axis=1)
    place = (jnp.arange(slots, dtype=jnp.int32)[:, None] == position[None, :]).astype(BF)
    tile_rows = NX // sky_count
    rows = (offset // NY).astype(BF)
    cols = (offset % NY).astype(BF)
    taps = KSIDE * KSIDE // gz_count
    own_taps = lax.dynamic_slice_in_dim(kernel, lax.axis_index("gz") * taps, taps, axis=1)
    wide = slab // 128 * 128
    main = jnp.dot(place, spectra[:, :wide], preferred_element_type=F32).astype(BF)
    rest = jnp.concatenate([spectra[:, wide:], own_taps, rows[:, None], cols[:, None]], axis=1)
    rest = lax.dot_general(rest, place, (((0,), (1,)), ((), ())), preferred_element_type=F32).astype(BF)
    per_row = -(-slots // wide)
    rest = jnp.pad(rest, ((0, -rest.shape[0] % 8), (0, per_row * wide - slots)))
    rest = rest.reshape(-1, wide)
    return jnp.concatenate([main, rest], axis=0), wide, per_row, cap


def shards(spectra, kernel, owner, offset):
    sky_count, gz_count = lax.axis_size("sky"), lax.axis_size("gz")
    slab = spectra.shape[1]
    tile_rows = NX // sky_count
    pad_rows = tile_rows + 8
    block, wide, per_row, cap = pack(spectra, kernel, owner, offset)
    slots = sky_count * cap
    got = lax.all_gather(block, ("sky", "gz"), axis=0, tiled=False)
    got = got.reshape(sky_count, gz_count, block.shape[0], wide)
    main = got[:, :, :slots].reshape(sky_count, gz_count, sky_count, cap, wide)
    main = main.transpose(2, 0, 3, 1, 4).reshape(sky_count, slots, gz_count * wide)
    rest = got[:, :, slots:].reshape(sky_count, gz_count, -1, per_row * wide)[:, :, :, :slots]
    rest = rest.reshape(sky_count, gz_count, -1, sky_count, cap)
    rest = rest.transpose(3, 0, 4, 1, 2).reshape(sky_count, slots, gz_count, -1)
    narrow = slab - wide
    taps = KSIDE * KSIDE // gz_count
    tail = rest[..., :narrow].reshape(sky_count, slots, gz_count * narrow)
    weights = rest[..., narrow : narrow + taps].reshape(sky_count, slots, KSIDE, KSIDE).astype(F32)
    row = rest[:, :, 0, narrow + taps].astype(jnp.int32)
    col = rest[:, :, 0, narrow + taps + 1].astype(jnp.int32)

    cos_w, sin_w = dft_tables(NW)
    table = np.concatenate([cos_w, -sin_w], axis=1).reshape(gz_count, slab, 2 * NW)
    table_main = jnp.asarray(table[:, :wide].reshape(gz_count * wide, 2 * NW), BF)
    table_tail = jnp.asarray(table[:, wide:].reshape(gz_count * narrow, 2 * NW), BF)
    lines = jnp.concatenate([main, tail], axis=-1)
    spec = jnp.einsum(
        "ojw,wv->ojv", lines, jnp.concatenate([table_main, table_tail]), preferred_element_type=F32
    ).astype(BF)

    per_block = NY // (sky_count * gz_count)
    first = (lax.axis_index("sky") * gz_count + lax.axis_index("gz")) * per_block
    freq = first + jnp.arange(per_block, dtype=jnp.int32)
    cells = col[:, None, :, None] + jnp.arange(KSIDE, dtype=jnp.int32)
    phase = (freq[None, :, None, None] * cells % NY).astype(F32) * (2.0 * math.pi / NY)
    factor = 1.0 / math.sqrt(NY)
    wave = jnp.stack([jnp.cos(phase), -jnp.sin(phase)], axis=1) * factor
    side = [
        sum(wave[..., b] * weights[:, None, None, :, a, b] for b in range(KSIDE))
        for a in range(KSIDE)
    ]
    lag = jnp.arange(pad_rows, dtype=jnp.int32)[None, :, None] - row[:, None, :]
    lag = lag[:, None, None]
    spread = sum(jnp.where(lag == a, side[a][:, :, :, None, :], 0.0) for a in range(KSIDE)).astype(BF)

    both = jnp.einsum("ozkrj,ojv->ozkrv", spread, spec, preferred_element_type=F32)
    plane_re = both[:, 0, ..., :NW] - both[:, 1, ..., NW:]
    plane_im = both[:, 0, ..., NW:] + both[:, 1, ..., :NW]
    planes = jnp.stack([plane_re, plane_im]).astype(BF)
    cos_x, sin_x = dft_tables(NX)
    held = (np.arange(sky_count)[:, None] * tile_rows + np.arange(pad_rows)[None, :]) % NX
    cos_x, sin_x = cos_x[held], sin_x[held]
    turn = np.stack([np.stack([cos_x, sin_x]), np.stack([-sin_x, cos_x])])
    return jnp.einsum("cokrv,zcoru->zukv", planes, jnp.asarray(turn, BF), preferred_element_type=F32)


def solution(mesh):
    in_specs = (P("sky", "gz"), P("sky", None), P("sky", None), P("sky"))
    out_specs = P(None, None, ("sky", "gz"), None)
    return jax.shard_map(shards, mesh=mesh, in_specs=in_specs, out_specs=out_specs, check_vma=False)
```

profile of v0, /device:TPU:9, one launch (start us, length us, event | category | flops | bytes accessed | tf_op | source)
XLA Modules:
  0.0 184.8 jit_solution(704391173075143215)
XLA Ops:
  6.5 0.9 convert_reduce_fusion
  7.5 0.7 multiply_add_fusion.4
  8.2 0.7 slice.112
  8.8 0.7 fusion.47
  9.6 1.1 convolution_convert_fusion
  10.7 0.2 convolution_convert_fusion.1
  10.9 0.7 pad_maximum_fusion.1
  11.6 0.0 all-gather.3.cloned.1.call-update
  11.7 68.4 %all-gather.3.cloned.1.call-done = bf16[10752,256]{1,0:T(8,128)(2,1)} async-done(((bf16[336,256]{1,0:T(8,128)(2,1)}), bf16[10752,256]{1,0:T(8,128)(2,1)}) %all-gather.3.cloned.1.call-update) | async-done | bytes 5505040 | tf_op jit(solution)/shard_map/all_gather | solution.py:56
  80.1 1.0 slice.144
  81.1 5.4 %slice.169 = bf16[8,4,320,256]{3,2,1,0:T(8,128)(2,1)} slice(bf16[8,4,336,256]{3,2,1,0:T(8,128)(2,1)} %bitcast.138), slice={[0:8], [0:4], [0:320], [0:256]} | slice | bytes 10485760 | tf_op jit(solution)/shard_map/slice | solution.py:58
  86.5 0.1 reshape.271
  86.6 0.4 reshape.272
  87.0 0.3 copy.34
  87.4 0.4 reshape.273
  87.9 11.5 %copy.35 = bf16[8,8,40,4,256]{4,3,2,1,0:T(4,128)(2,1)} copy(bf16[8,8,40,4,256]{4,2,0,3,1:T(8,128)(2,1)} %bitcast.136) | data formatting | bytes 10485760 | tf_op jit(solution)/shard_map/transpose | solution.py:59
  99.4 9.3 %reshape.275 = bf16[8,320,1024]{2,1,0:T(8,128)(2,1)} reshape(bf16[8,8,40,4,256]{4,3,2,1,0:T(4,128)(2,1)} %copy.35) | data formatting | bytes 10485760 | tf_op jit(solution)/shard_map/reshape | solution.py:59
  108.8 0.1 fusion.52
  109.0 0.3 fusion.30
  109.2 0.3 copy.37
  109.7 1.6 fusion.35
  111.3 0.1 maximum_multiply_fusion
  111.4 18.6 %fusion.66 = bf16[8,320,2064,1,1]{2,1,4,3,0:T(8,128)(2,1)S(1)} fusion(bf16[1032,2064,1]{1,0,2:T(8,128)(2,1)} %constant.81, bf16[8,320,8]{2,1,0:T(8,128)(2,1)S(1)} %copy.37, bf16[8,320,1024]{2,1,0:T(8,128)(2,1)} %reshape.275), kind=kOutput, calls=%fused_computation.11.clone.2 | convolution fusion | flops 10921697280 | bytes 20111616 | tf_op jit(solution)/shard_map/ojw,wv->ojv/dot_general | solution.py:75
  130.0 0.1 multiply_add_fusion.2
  130.1 0.1 multiply_add_fusion.3
  130.2 18.7 %fusion.5 = f32[8,2,8,40,2064]{4,3,2,1,0:T(8,128)} fusion(f32[8,2,8,320]{3,2,1,0:T(8,128)S(1)} %get-tuple-element.6, f32[8,2,8,320]{3,2,1,0:T(8,128)S(1)} %get-tuple-element.8, f32[8,2,8,320]{3,2,1,0:T(8,128)S(1)} %get-tuple-element.7, f32[8,2,8,320]{3,2,1,0:T(8,128)S(1)} %get-tuple-element.5, pred[8,40,320]{2,1,0:T(8,128)(4,1)S(1)} %get-tuple-element.30, ...), kind=kOutput, calls=%fused_computation.10 | convolution fusion | flops 6776422400 | bytes 53903360 | tf_op jit(solution)/shard_map/ozkrj,ojv->ozkrv/dot_general | solution.py:94
  148.9 9.1 %fusion.11 = bf16[1,8,8,40,1032]{4,3,2,1,0:T(8,128)(2,1)S(1)} fusion(f32[8,2,8,40,2064]{4,3,2,1,0:T(8,128)} %fusion.5), kind=kLoop, calls=%fused_computation.16 | loop fusion | flops 5283840 | bytes 26419200 | tf_op jit(solution)/shard_map/add | solution.py:96
  158.0 0.0 copy-start.2
  158.0 9.1 %fusion.10 = bf16[1,8,8,40,1032]{4,3,2,1,0:T(8,128)(2,1)S(1)} fusion(f32[8,2,8,40,2064]{4,3,2,1,0:T(8,128)} %fusion.5), kind=kLoop, calls=%fused_computation.15 | loop fusion | flops 5283840 | bytes 26419200 | tf_op jit(solution)/shard_map/sub | solution.py:95
  167.2 0.0 copy-start.1
  167.2 10.7 %convolution_bitcast_fusion = f32[2,256,8,1032]{1,3,2,0:T(8,128)} fusion(bf16[2,2,8,40,256,1]{4,3,2,1,5,0:T(8,128)(2,1)S(1)} %copy-done.2, bf16[1,8,8,40,1032]{4,3,2,1,0:T(8,128)(2,1)S(1)} %fusion.11, bf16[1,8,8,40,1032]{4,3,2,1,0:T(8,128)(2,1)S(1)} %fusion.10), kind=kOutput, calls=%fused_computation | convolution fusion | flops 5415936000 | bytes 28131328 | tf_op jit(solution)/shard_map/cokrv,zcoru->zukv/dot_general | solution.py:102
  177.9 0.0 copy-done.1
  (25 shorter events, 0.3 us)
Async XLA Ops:
  6.5 4.2 %copy-start = (bf16[256,16]{0,1:T(8,128)(2,1)S(1)}, bf16[256,16]{0,1:T(8,128)(2,1)}, u32[]{:S(2)}) copy-start(bf16[256,16]{0,1:T(8,128)(2,1)} %param.8) | copy-start | bytes 24580
  6.5 73.6 %all-gather.3.cloned.1.call-start = ((), (), s32[]{:S(2)}) async-start(), calls=%async_computation | async-start | bytes 5677056 | tf_op jit(solution)/shard_map/all_gather | solution.py:56
  158.0 9.2 %copy-start.2 = (bf16[2,2,8,40,256,1]{4,3,2,1,5,0:T(8,128)(2,1)S(1)}, bf16[2,2,8,40,256,1]{4,3,2,1,5,0:T(8,128)(2,1)}, u32[]{:S(2)}) copy-start(bf16[2,2,8,40,256,1]{4,3,2,1,5,0:T(8,128)(2,1)} %constant.80) | copy-start | bytes 1966084
  167.2 10.8 %copy-start.1 = (bf16[256,16]{0,1:T(8,128)(2,1)S(1)}, bf16[256,16]{0,1:T(8,128)(2,1)}, u32[]{:S(2)}) copy-start(bf16[256,16]{0,1:T(8,128)(2,1)} %param.8) | copy-start | bytes 24580
Sparse Core Ops, SparseCore 0:
  11.8 68.2 all-gather.2
where the time goes:
time: 186 us; the launch traced here: 185 us
  waiting for transfers between devices  68.4 us (37%)
  matrix products  49.3 us (27%)
  local copies, waits for them, and re-layouts  29.8 us (16%)
  other arithmetic  23.5 us (13%)
  between operations  13.7 us (7%)
    all_gather x1, waiting for transfers between devices, shards(): got = lax.all_gather(block, ('sky', 'gz'), axis=0, tiled=False)  68.4 us
    dot_general x1, matrix products, shards(): jnp.einsum('ozkrj,ojv->ozkrv', spread, spec, preferred_element_type=F32)  18.7 us
    dot_general x1, matrix products, shards(): jnp.einsum('ojw,wv->ojv', lines, jnp.concatenate([table_main, table_tail]...  18.6 us
    transpose x1, local copies, waits for them, and re-layouts, shards(): main.transpose(2, 0, 3, 1, 4).reshape(sky_count, slots, gz_count * wide)  11.5 us
    dot_general x1, matrix products, shards(): jnp.einsum('cokrv,zcoru->zukv', planes, jnp.asarray(turn, BF), preferred_...  10.7 us
    reshape x1, local copies, waits for them, and re-layouts, shards(): main.transpose(2, 0, 3, 1, 4).reshape(sky_count, slots, gz_count * wide)  9.34 us
    sub x1, other arithmetic, shards(): plane_re = both[:, 0, ..., :NW] - both[:, 1, ..., NW:]  9.15 us
    add x1, other arithmetic, shards(): plane_im = both[:, 0, ..., NW:] + both[:, 1, ..., :NW]  9.09 us
  transfers between devices with their start and end apart: 1, of which 1 were waited for; matrix products, arithmetic and copies ran while one was open for 0% of the time, Pallas kernels for 0%

commit v1 on v0

v1 whole, which is shorter than its diff:
```python
import functools
import math

import jax
import jax.numpy as jnp
import numpy as np
from jax import lax
from jax.experimental import pallas as pl
from jax.experimental.pallas import tpu as pltpu
from jax.sharding import PartitionSpec as P

NX = 256
NY = 256
NW = 1032
KSIDE = 4
BF = jnp.bfloat16
F32 = jnp.float32
LANES = 128
INTERPRET = False


def dft_tables(length):
    steps = np.arange(length)
    angles = (steps[:, None] * steps[None, :] % length).astype(np.float64) * (2.0 * math.pi / length)
    factor = 1.0 / math.sqrt(length)
    return np.cos(angles) * factor, np.sin(angles) * factor


def pack(spectra, kernel, owner, offset):
    sky_count, gz_count = lax.axis_size("sky"), lax.axis_size("gz")
    fibre_count, slab = spectra.shape
    cap = -(-(fibre_count * 5 // (4 * sky_count)) // 8) * 8
    slots = sky_count * cap
    own = owner[:, 0]
    order = jnp.arange(fibre_count, dtype=jnp.int32)
    earlier = (own[None, :] == own[:, None]) & (order[None, :] < order[:, None])
    position = own * cap + jnp.sum(earlier.astype(jnp.int32), axis=1)
    place = (jnp.arange(slots, dtype=jnp.int32)[:, None] == position[None, :]).astype(BF)
    tile_rows = NX // sky_count
    rows = (offset // NY).astype(BF)
    cols = (offset % NY).astype(BF)
    taps = KSIDE * KSIDE // gz_count
    own_taps = lax.dynamic_slice_in_dim(kernel, lax.axis_index("gz") * taps, taps, axis=1)
    wide = slab // 128 * 128
    main = jnp.dot(place, spectra[:, :wide], preferred_element_type=F32).astype(BF)
    rest = jnp.concatenate([spectra[:, wide:], own_taps, rows[:, None], cols[:, None]], axis=1)
    rest = lax.dot_general(rest, place, (((0,), (1,)), ((), ())), preferred_element_type=F32).astype(BF)
    per_row = -(-slots // wide)
    rest = jnp.pad(rest, ((0, -rest.shape[0] % 8), (0, per_row * wide - slots)))
    rest = rest.reshape(-1, wide)
    return jnp.concatenate([main, rest], axis=0), wide, per_row, cap


def cube_kernel(dims, got_ref, tail_ref, wave_ref, spread_ref, turn_ref, out_ref, spec_ref, plane_ref):
    sky_count, gz_count, cap, wide, tile_rows, pad_rows, freqs = dims
    slots = sky_count * cap
    depth = gz_count * wide

    def transform(source, _):
        spec = jnp.dot(tail_ref[source], wave_ref[0, depth:], preferred_element_type=F32)
        for g in range(gz_count):
            lines = got_ref[source * gz_count + g, :slots, :]
            table = wave_ref[0, g * wide : (g + 1) * wide, :]
            spec = spec + jnp.dot(lines, table, preferred_element_type=F32)
        for o in range(sky_count):
            spec_ref[o, source] = spec[o * cap : (o + 1) * cap]
        return _

    lax.fori_loop(0, sky_count, transform, 0)
    plane_ref[:, :8] = jnp.zeros((freqs, 8, 2 * LANES), F32)

    def spread_out(o, _):
        spec = spec_ref[o].reshape(slots, 2 * LANES).astype(BF)
        both = jnp.dot(spread_ref[o], spec, preferred_element_type=F32)
        half = freqs * pad_rows
        first = pl.multiple_of(o * tile_rows, 8)
        for k in range(freqs):
            by_re = both[k * pad_rows : (k + 1) * pad_rows]
            by_im = both[half + k * pad_rows : half + (k + 1) * pad_rows]
            here = jnp.concatenate(
                [by_re[:, :LANES] - by_im[:, LANES:], by_re[:, LANES:] + by_im[:, :LANES]], axis=1
            )
            plane_ref[k, pl.ds(first, 8)] += here[:8]
            plane_ref[k, pl.ds(first + 8, tile_rows)] = here[8:]
        return _

    lax.fori_loop(0, sky_count, spread_out, 0)
    for k in range(freqs):
        plane_ref[k, :8] += plane_ref[k, NX : NX + 8]
        turned = jnp.dot(turn_ref[...], plane_ref[k, :NX].astype(BF), preferred_element_type=F32)
        out_ref[pl.ds(k, NX, stride=freqs), :] = turned[:NX, :LANES] + turned[NX:, LANES:]
        out_ref[pl.ds(NX * freqs + k, NX, stride=freqs), :] = turned[:NX, LANES:] - turned[NX:, :LANES]


def shards(spectra, kernel, owner, offset):
    sky_count, gz_count = lax.axis_size("sky"), lax.axis_size("gz")
    slab = spectra.shape[1]
    tile_rows = NX // sky_count
    pad_rows = tile_rows + 8
    block, wide, per_row, cap = pack(spectra, kernel, owner, offset)
    slots = sky_count * cap
    got = lax.all_gather(block, ("sky", "gz"), axis=0, tiled=False)
    rest = got[:, slots:].reshape(sky_count, gz_count, -1, per_row * wide)[:, :, :, :slots]
    narrow = slab - wide
    taps = KSIDE * KSIDE // gz_count
    tail = rest[:, :, :narrow].reshape(sky_count, gz_count * narrow, slots).transpose(0, 2, 1)

    def by_owner(item):
        item = item.reshape(-1, sky_count, cap).reshape(sky_count, -1, sky_count, cap)
        return item.transpose(2, 1, 0, 3).reshape(sky_count, -1, slots)

    weights = by_owner(rest[:, :, narrow : narrow + taps]).astype(F32)
    row = by_owner(rest[:, 0, narrow + taps])[:, 0].astype(jnp.int32)
    col = by_owner(rest[:, 0, narrow + taps + 1])[:, 0].astype(jnp.int32)

    per_block = NY // (sky_count * gz_count)
    first = (lax.axis_index("sky") * gz_count + lax.axis_index("gz")) * per_block
    freq = first + jnp.arange(per_block, dtype=jnp.int32)
    factor = 1.0 / math.sqrt(NY)
    side = [0.0] * KSIDE
    for b in range(KSIDE):
        phase = (freq[None, :, None] * (col + b)[:, None, :] % NY).astype(F32) * (2.0 * math.pi / NY)
        wave = jnp.stack([jnp.cos(phase), -jnp.sin(phase)], axis=1) * factor
        for a in range(KSIDE):
            side[a] = side[a] + wave * weights[:, None, None, a * KSIDE + b]
    lag = jnp.arange(pad_rows, dtype=jnp.int32)[None, :, None] - row[:, None, :]
    lag = lag[:, None, None]
    spread = jnp.zeros((), F32)
    for a in range(KSIDE):
        spread = jnp.where(lag == a, side[a][:, :, :, None, :], spread)
    spread = spread.astype(BF).reshape(sky_count, 2 * per_block * pad_rows, slots)

    chunks = -(-NW // LANES)
    cos_w, sin_w = dft_tables(NW)
    wave_table = np.zeros((NW, 2, chunks * LANES), np.float32)
    wave_table[:, 0, :NW], wave_table[:, 1, :NW] = cos_w, -sin_w
    wave_table = wave_table.reshape(gz_count, slab, 2, chunks, LANES)
    wave_table = np.concatenate(
        [
            wave_table[:, :wide].reshape(gz_count * wide, 2, chunks, LANES),
            wave_table[:, wide:].reshape(gz_count * narrow, 2, chunks, LANES),
        ]
    )
    wave_table = wave_table.transpose(2, 0, 1, 3).reshape(chunks, NW, 2 * LANES)
    turn = np.concatenate(dft_tables(NX))

    dims = (sky_count, gz_count, cap, wide, tile_rows, pad_rows, per_block)
    macs = chunks * 2 * LANES * sky_count * slots * (NW + 2 * per_block * pad_rows)
    macs += chunks * 2 * LANES * 2 * NX * NX * per_block
    result = pl.pallas_call(
        functools.partial(cube_kernel, dims),
        grid=(chunks,),
        in_specs=[
            pl.BlockSpec(got.shape, lambda i: (0, 0, 0)),
            pl.BlockSpec(tail.shape, lambda i: (0, 0, 0)),
            pl.BlockSpec((1, NW, 2 * LANES), lambda i: (i, 0, 0)),
            pl.BlockSpec(spread.shape, lambda i: (0, 0, 0)),
            pl.BlockSpec(turn.shape, lambda i: (0, 0)),
        ],
        out_specs=pl.BlockSpec((2 * NX * per_block, LANES), lambda i: (0, i)),
        out_shape=jax.ShapeDtypeStruct((2 * NX * per_block, NW), F32),
        scratch_shapes=[
            pltpu.VMEM((sky_count, sky_count, cap, 2 * LANES), F32),
            pltpu.VMEM((per_block, NX + 8, 2 * LANES), F32),
        ],
        compiler_params=pltpu.CompilerParams(vmem_limit_bytes=56 * 1024 * 1024),
        cost_estimate=pl.CostEstimate(flops=2 * macs, bytes_accessed=32 * 1024 * 1024, transcendentals=0),
        interpret=INTERPRET,
    )(got, tail, jnp.asarray(wave_table, BF), spread, jnp.asarray(turn, BF))
    return result.reshape(2, NX, per_block, NW)


def solution(mesh):
    in_specs = (P("sky", "gz"), P("sky", None), P("sky", None), P("sky"))
    out_specs = P(None, None, ("sky", "gz"), None)
    return jax.shard_map(shards, mesh=mesh, in_specs=in_specs, out_specs=out_specs, check_vma=False)
```

time: 186 us -> 178 us (0.957)
  Pallas kernels: 0 us -> 62.3 us
  matrix products: 49.3 us -> 1.32 us
  other arithmetic: 23.5 us -> 9.52 us
  local copies, waits for them, and re-layouts: 29.8 us -> 22.1 us
    pallas_call x0 -> x1, Pallas kernels: none -> 62.3 us  [shards(): pl.pallas_call(functools.partial(cube_kernel, dims), grid=(chunks,), in_s...]
    dot_general x3 -> x0, matrix products: 48 us -> none  [the longest x1 18.7 us: shards(): jnp.einsum('ozkrj,ojv->ozkrv', spread, spec, preferred_element_type=F32)]
    transpose x2 -> x0, local copies, waits for them, and re-layouts: 11.9 us -> none  [the longest x1 11.5 us: shards(): main.transpose(2, 0, 3, 1, 4).reshape(sky_count, slots, gz_count * wide)]
    sub x1 -> x0, other arithmetic: 9.15 us -> none  [shards(): plane_re = both[:, 0, ..., :NW] - both[:, 1, ..., NW:]]
    add x4 -> x5, other arithmetic: 9.34 us -> 0.33 us  [the longest x4 0.33 us: shards(): side[a] = side[a] + wave * weights[:, None, None, a * KSIDE + b]]
    reshape x5 -> x3, local copies, waits for them, and re-layouts: 10.6 us -> 19.4 us  [the longest x1 18.2 us: shards(): return result.reshape(2, NX, per_block, NW)]
    slice x6 -> x4, local copies, waits for them, and re-layouts: 6.57 us -> 1.08 us  [the longest x1 0.97 us: shards(): got[:, slots:].reshape(sky_count, gz_count, -1, per_row * wide)]
    another operation x0 -> x1, other arithmetic: none -> 4.08 us
where the time goes in v1:
time: 178 us; the launch traced here: 177 us
  waiting for transfers between devices  68.4 us (38%)
  Pallas kernels  62.3 us (35%)
  local copies, waits for them, and re-layouts  22.1 us (12%)
  between operations  13.6 us (8%)
  other arithmetic  9.52 us (5%)
    all_gather x1, waiting for transfers between devices, shards(): got = lax.all_gather(block, ('sky', 'gz'), axis=0, tiled=False)  68.4 us
    pallas_call x1, Pallas kernels, shards(): pl.pallas_call(functools.partial(cube_kernel, dims), grid=(chunks,), in_s...  62.3 us
    reshape x1, local copies, waits for them, and re-layouts, shards(): return result.reshape(2, NX, per_block, NW)  18.2 us
    another operation x1, other arithmetic  4.08 us
  transfers between devices with their start and end apart: 1, of which 1 were waited for; matrix products, arithmetic and copies ran while one was open for 0% of the time, Pallas kernels for 0%

profile of v1, /device:TPU:9, one launch (start us, length us, event | category | flops | bytes accessed | tf_op | source)
XLA Modules:
  0.0 177.3 jit_solution(13102445634889655073)
XLA Ops:
  6.5 0.0 copy-start
  6.5 0.0 all-gather.3.cloned.1.call-start
  6.5 0.9 convert_reduce_fusion
  7.5 0.7 multiply_add_fusion.4
  8.2 0.7 slice.75
  8.8 0.7 fusion.32
  9.6 1.1 convolution_convert_fusion
  10.7 0.2 convolution_convert_fusion.1
  10.9 0.7 pad_maximum_fusion.4
  11.6 0.0 all-gather.3.cloned.1.call-update
  11.7 68.4 %all-gather.3.cloned.1.call-done = bf16[10752,256]{1,0:T(8,128)(2,1)} async-done(((bf16[336,256]{1,0:T(8,128)(2,1)}), bf16[10752,256]{1,0:T(8,128)(2,1)}) %all-gather.3.cloned.1.call-update) | async-done | bytes 5505040 | tf_op jit(solution)/shard_map/all_gather | solution.py:102
  80.1 1.0 slice.97
  81.1 0.1 reshape.530
  81.2 0.1 slice.101
  81.3 0.1 reshape.537
  81.4 0.1 reshape.534
  81.5 0.1 reshape.536
  81.6 0.1 reshape.533
  81.7 0.2 reshape.538
  81.9 0.1 copy.28
  82.0 0.2 reshape.535
  82.2 0.2 slice_multiply_fusion.15
  82.4 0.3 fusion.3
  82.7 1.2 copy.22
  84.0 1.6 fusion.23
  85.6 0.1 multiply_add_fusion.2
  85.7 0.1 multiply_add_fusion.1
  85.8 0.1 multiply_add_fusion
  85.8 0.1 multiply_add_fusion.3
  85.9 4.1 %select_convert_fusion = bf16[8,2,8,40,320]{4,3,2,1,0:T(8,128)(2,1)} fusion(bf16[8,2,8,320]{3,2,1,0:T(8,128)(2,1)S(1)} %multiply_add_fusion, bf16[8,2,8,320]{3,2,1,0:T(8,128)(2,1)S(1)} %multiply_add_fusion.1, bf16[8,2,8,320]{3,2,1,0:T(8,128)(2,1)S(1)} %multiply_add_fusion.2, bf16[8,2,8,320]{3,2,1,0:T(8,128)(2,1)S(1)} %multiply_add_fusion.3, ...), kind=kLoop, calls=%fused_computation | loop fusion | flops 6553600 | bytes 4014080 | tf_op jit(solution)/shard_map/convert.9
  90.0 62.3 %shard_map.64 = f32[4096,1032]{1,0:T(8,128)} custom-call(bf16[32,336,256]{2,1,0:T(8,128)(2,1)} %bitcast.71, bf16[8,320,8]{2,1,0:T(8,128)(2,1)} %bitcast.66, bf16[9,1032,256]{2,1,0:T(8,128)(2,1)} %constant.89.clone.wave_ref, bf16[8,640,320]{2,1,0:T(8,128)(2,1)} %bitcast.64, bf16[512,256]{1,0:T(8,128)(2,1)} %constant.90.clone.turn_ref), custom_call_target="tpu_custom_call" | custom-call | flops 24555552768 | bytes 33554432 | tf_op jit(solution)/shard_map/pallas_call | solution.py:150
  152.3 18.2 %copy.29 = f32[2,256,8,1032]{1,3,2,0:T(8,128)} copy(f32[2,256,8,1032]{3,2,1,0:T(8,128)} %bitcast.63) | data formatting | bytes 33816576 | tf_op jit(solution)/shard_map/reshape | solution.py:170
  (23 shorter events, 0.2 us)
Async XLA Ops:
  6.5 4.2 %copy-start = (bf16[256,16]{0,1:T(8,128)(2,1)S(1)}, bf16[256,16]{0,1:T(8,128)(2,1)}, u32[]{:S(2)}) copy-start(bf16[256,16]{0,1:T(8,128)(2,1)} %param.7) | copy-start | bytes 24580
  6.5 73.6 %all-gather.3.cloned.1.call-start = ((), (), s32[]{:S(2)}) async-start(), calls=%async_computation | async-start | bytes 5677056 | tf_op jit(solution)/shard_map/all_gather | solution.py:102
Sparse Core Ops, SparseCore 0:
  11.8 68.2 all-gather.2

commit v2 on v1

--- a/solution.py
+++ b/solution.py
@@ -15,7 +15,7 @@
 KSIDE = 4
 BF = jnp.bfloat16
 F32 = jnp.float32
-LANES = 128
+WIDTH = 384
 INTERPRET = False
 
 
@@ -55,22 +55,32 @@
     sky_count, gz_count, cap, wide, tile_rows, pad_rows, freqs = dims
     slots = sky_count * cap
     depth = gz_count * wide
+    pair = 2
 
-    def transform(source, _):
-        spec = jnp.dot(tail_ref[source], wave_ref[0, depth:], preferred_element_type=F32)
-        for g in range(gz_count):
-            lines = got_ref[source * gz_count + g, :slots, :]
-            table = wave_ref[0, g * wide : (g + 1) * wide, :]
-            spec = spec + jnp.dot(lines, table, preferred_element_type=F32)
-        for o in range(sky_count):
-            spec_ref[o, source] = spec[o * cap : (o + 1) * cap]
+    def transform(step, _):
+        lines = jnp.concatenate(
+            [
+                jnp.concatenate(
+                    [got_ref[(step * pair + i) * gz_count + g, :slots, :] for i in range(pair)], axis=0
+                )
+                for g in range(gz_count)
+            ],
+            axis=1,
+        )
+        tail = jnp.concatenate([tail_ref[step * pair + i] for i in range(pair)], axis=0)
+        spec = jnp.dot(lines, wave_ref[0, :depth], preferred_element_type=F32)
+        spec = spec + jnp.dot(tail, wave_ref[0, depth:], preferred_element_type=F32)
+        for i in range(pair):
+            for o in range(sky_count):
+                start = i * slots + o * cap
+                spec_ref[o, step * pair + i] = spec[start : start + cap]
         return _
 
-    lax.fori_loop(0, sky_count, transform, 0)
-    plane_ref[:, :8] = jnp.zeros((freqs, 8, 2 * LANES), F32)
+    lax.fori_loop(0, sky_count // pair, transform, 0)
+    plane_ref[:, :8] = jnp.zeros((freqs, 8, 2 * WIDTH), F32)
 
     def spread_out(o, _):
-        spec = spec_ref[o].reshape(slots, 2 * LANES).astype(BF)
+        spec = spec_ref[o].reshape(slots, 2 * WIDTH).astype(BF)
         both = jnp.dot(spread_ref[o], spec, preferred_element_type=F32)
         half = freqs * pad_rows
         first = pl.multiple_of(o * tile_rows, 8)
@@ -78,18 +88,25 @@
             by_re = both[k * pad_rows : (k + 1) * pad_rows]
             by_im = both[half + k * pad_rows : half + (k + 1) * pad_rows]
             here = jnp.concatenate(
-                [by_re[:, :LANES] - by_im[:, LANES:], by_re[:, LANES:] + by_im[:, :LANES]], axis=1
+                [by_re[:, :WIDTH] - by_im[:, WIDTH:], by_re[:, WIDTH:] + by_im[:, :WIDTH]], axis=1
             )
             plane_ref[k, pl.ds(first, 8)] += here[:8]
             plane_ref[k, pl.ds(first + 8, tile_rows)] = here[8:]
         return _
 
     lax.fori_loop(0, sky_count, spread_out, 0)
-    for k in range(freqs):
+
+    def turn_rows(k, _):
         plane_ref[k, :8] += plane_ref[k, NX : NX + 8]
-        turned = jnp.dot(turn_ref[...], plane_ref[k, :NX].astype(BF), preferred_element_type=F32)
-        out_ref[pl.ds(k, NX, stride=freqs), :] = turned[:NX, :LANES] + turned[NX:, LANES:]
-        out_ref[pl.ds(NX * freqs + k, NX, stride=freqs), :] = turned[:NX, LANES:] - turned[NX:, :LANES]
+        plane = plane_ref[k, :NX].astype(BF)
+        turned = lax.dot_general(
+            plane, turn_ref[...], (((0,), (0,)), ((), ())), preferred_element_type=F32
+        )
+        out_ref[0, k] = turned[:WIDTH, :NX] + turned[WIDTH:, NX:]
+        out_ref[1, k] = turned[WIDTH:, :NX] - turned[:WIDTH, NX:]
+        return _
+
+    lax.fori_loop(0, freqs, turn_rows, 0)
 
 
 def shards(spectra, kernel, owner, offset):
@@ -130,44 +147,44 @@
         spread = jnp.where(lag == a, side[a][:, :, :, None, :], spread)
     spread = spread.astype(BF).reshape(sky_count, 2 * per_block * pad_rows, slots)
 
-    chunks = -(-NW // LANES)
+    chunks = -(-NW // WIDTH)
     cos_w, sin_w = dft_tables(NW)
-    wave_table = np.zeros((NW, 2, chunks * LANES), np.float32)
+    wave_table = np.zeros((NW, 2, chunks * WIDTH), np.float32)
     wave_table[:, 0, :NW], wave_table[:, 1, :NW] = cos_w, -sin_w
-    wave_table = wave_table.reshape(gz_count, slab, 2, chunks, LANES)
+    wave_table = wave_table.reshape(gz_count, slab, 2, chunks, WIDTH)
     wave_table = np.concatenate(
         [
-            wave_table[:, :wide].reshape(gz_count * wide, 2, chunks, LANES),
-            wave_table[:, wide:].reshape(gz_count * narrow, 2, chunks, LANES),
+            wave_table[:, :wide].reshape(gz_count * wide, 2, chunks, WIDTH),
+            wave_table[:, wide:].reshape(gz_count * narrow, 2, chunks, WIDTH),
         ]
     )
-    wave_table = wave_table.transpose(2, 0, 1, 3).reshape(chunks, NW, 2 * LANES)
-    turn = np.concatenate(dft_tables(NX))
+    wave_table = wave_table.transpose(2, 0, 1, 3).reshape(chunks, NW, 2 * WIDTH)
+    turn = np.concatenate(dft_tables(NX), axis=1)
 
     dims = (sky_count, gz_count, cap, wide, tile_rows, pad_rows, per_block)
-    macs = chunks * 2 * LANES * sky_count * slots * (NW + 2 * per_block * pad_rows)
-    macs += chunks * 2 * LANES * 2 * NX * NX * per_block
+    macs = chunks * 2 * WIDTH * sky_count * slots * (NW + 2 * per_block * pad_rows)
+    macs += chunks * 2 * WIDTH * 2 * NX * NX * per_block
     result = pl.pallas_call(
         functools.partial(cube_kernel, dims),
         grid=(chunks,),
         in_specs=[
-            pl.BlockSpec(got.shape, lambda i: (0, 0, 0)),
-            pl.BlockSpec(tail.shape, lambda i: (0, 0, 0)),
-            pl.BlockSpec((1, NW, 2 * LANES), lambda i: (i, 0, 0)),
-            pl.BlockSpec(spread.shape, lambda i: (0, 0, 0)),
+            pl.BlockSpec(got.shape, lambda i: (0, 0, 0), pipeline_mode=pl.Buffered(1)),
+            pl.BlockSpec(tail.shape, lambda i: (0, 0, 0), pipeline_mode=pl.Buffered(1)),
+            pl.BlockSpec((1, NW, 2 * WIDTH), lambda i: (i, 0, 0)),
+            pl.BlockSpec(spread.shape, lambda i: (0, 0, 0), pipeline_mode=pl.Buffered(1)),
             pl.BlockSpec(turn.shape, lambda i: (0, 0)),
         ],
-        out_specs=pl.BlockSpec((2 * NX * per_block, LANES), lambda i: (0, i)),
-        out_shape=jax.ShapeDtypeStruct((2 * NX * per_block, NW), F32),
+        out_specs=pl.BlockSpec((2, per_block, WIDTH, NX), lambda i: (0, 0, i, 0)),
+        out_shape=jax.ShapeDtypeStruct((2, per_block, NW, NX), F32),
         scratch_shapes=[
-            pltpu.VMEM((sky_count, sky_count, cap, 2 * LANES), F32),
-            pltpu.VMEM((per_block, NX + 8, 2 * LANES), F32),
+            pltpu.VMEM((sky_count, sky_count, cap, 2 * WIDTH), F32),
+            pltpu.VMEM((per_block, NX + 8, 2 * WIDTH), F32),
         ],
         compiler_params=pltpu.CompilerParams(vmem_limit_bytes=56 * 1024 * 1024),
         cost_estimate=pl.CostEstimate(flops=2 * macs, bytes_accessed=32 * 1024 * 1024, transcendentals=0),
         interpret=INTERPRET,
     )(got, tail, jnp.asarray(wave_table, BF), spread, jnp.asarray(turn, BF))
-    return result.reshape(2, NX, per_block, NW)
+    return result.transpose(0, 3, 1, 2)
 
 
 def solution(mesh):

time: 178 us -> 147 us (0.83)
  local copies, waits for them, and re-layouts: 22.1 us -> 3.89 us
  Pallas kernels: 62.3 us -> 49.7 us
    reshape x1 -> x0, local copies, waits for them, and re-layouts: 18.2 us -> none  [shards(): return result.reshape(2, NX, per_block, NW)]
    pallas_call x1, Pallas kernels: 62.3 us -> 49.7 us  [shards(): pl.pallas_call(functools.partial(cube_kernel, dims), grid=(chunks,), in_s...]
where the time goes in v2:
time: 147 us
  waiting for transfers between devices  68.4 us (47%)
  Pallas kernels  49.7 us (34%)
  between operations  13.6 us (9%)
  other arithmetic  9.6 us (7%)
  local copies, waits for them, and re-layouts  3.89 us (3%)
    all_gather x1, waiting for transfers between devices, shards(): got = lax.all_gather(block, ('sky', 'gz'), axis=0, tiled=False)  68.4 us
    pallas_call x1, Pallas kernels, shards(): pl.pallas_call(functools.partial(cube_kernel, dims), grid=(chunks,), in_s...  49.7 us
    another operation x1, other arithmetic  4.16 us
  transfers between devices with their start and end apart: 1, of which 1 were waited for; matrix products, arithmetic and copies ran while one was open for 0% of the time, Pallas kernels for 0%

profile of v2, /device:TPU:9, one launch (start us, length us, event | category | flops | bytes accessed | tf_op | source)
XLA Modules:
  0.0 146.5 jit_solution(849061406335619725)
XLA Ops:
  6.5 0.0 copy-start
  6.5 0.0 all-gather.3.cloned.1.call-start
  6.5 0.9 convert_reduce_fusion
  7.5 0.7 multiply_add_fusion.4
  8.2 0.7 slice.75
  8.8 0.7 fusion.32
  9.6 1.1 convolution_convert_fusion
  10.7 0.0 copy-done
  10.7 0.2 convolution_convert_fusion.1
  10.9 0.7 pad_maximum_fusion.4
  11.6 0.0 all-gather.3.cloned.1.call-update
  11.7 68.4 %all-gather.3.cloned.1.call-done = bf16[10752,256]{1,0:T(8,128)(2,1)} async-done(((bf16[336,256]{1,0:T(8,128)(2,1)}), bf16[10752,256]{1,0:T(8,128)(2,1)}) %all-gather.3.cloned.1.call-update) | async-done | bytes 5505040 | tf_op jit(solution)/shard_map/all_gather | solution.py:119
  80.1 1.0 slice.97
  81.1 0.1 reshape.527
  81.2 0.1 slice.101
  81.3 0.1 reshape.533
  81.4 0.1 reshape.530
  81.5 0.1 reshape.532
  81.6 0.1 reshape.529
  81.7 0.2 reshape.534
  81.9 0.1 copy.25
  82.0 0.2 reshape.531
  82.2 0.2 slice_multiply_fusion.15
  82.4 0.3 fusion.3
  82.7 1.1 copy.19
  83.9 1.6 %fusion.23 = (f32[8,1,8,320]{3,2,1,0:T(8,128)S(1)}, f32[8,1,8,320]{3,2,1,0:T(8,128)S(1)}, f32[8,1,8,320]{3,2,1,0:T(8,128)S(1)}, f32[8,1,8,320]{3,2,1,0:T(8,128)S...) fusion(s32[8,320]{1,0:T(8,128)S(1)} %reshape.530, ...), kind=kLoop, calls=%fused_computation.64 | loop fusion | flops 1228800 | bytes 696352 | tf_op jit(solution)/shard_map/cos | solution.py:140
  85.5 0.1 multiply_add_fusion.2
  85.6 0.1 multiply_add_fusion.1
  85.7 0.1 multiply_add_fusion
  85.8 0.1 multiply_add_fusion.3
  85.9 4.2 %select_convert_fusion = bf16[8,2,8,40,320]{4,3,2,1,0:T(8,128)(2,1)} fusion(bf16[8,2,8,320]{3,2,1,0:T(8,128)(2,1)S(1)} %multiply_add_fusion, bf16[8,2,8,320]{3,2,1,0:T(8,128)(2,1)S(1)} %multiply_add_fusion.1, bf16[8,2,8,320]{3,2,1,0:T(8,128)(2,1)S(1)} %multiply_add_fusion.2, bf16[8,2,8,320]{3,2,1,0:T(8,128)(2,1)S(1)} %multiply_add_fusion.3, ...), kind=kLoop, calls=%fused_computation | loop fusion | flops 6553600 | bytes 4014080 | tf_op jit(solution)/shard_map/convert.9
  90.0 49.7 %shard_map.64 = f32[2,8,1032,256]{3,2,1,0:T(8,128)} custom-call(bf16[32,336,256]{2,1,0:T(8,128)(2,1)} %bitcast.70, bf16[8,320,8]{2,1,0:T(8,128)(2,1)} %bitcast.65, bf16[3,1032,768]{2,1,0:T(8,128)(2,1)} %constant.89.clone.wave_ref, bf16[8,640,320]{2,1,0:T(8,128)(2,1)} %bitcast.63, bf16[256,512]{1,0:T(8,128)(2,1)} %constant.90.clone.turn_ref), custom_call_target="tpu_custom_call" | custom-call | flops 24555552768 | bytes 33554432 | tf_op jit(solution)/shard_map/pallas_call | solution.py:167
  (22 shorter events, 0.2 us)
Async XLA Ops:
  6.5 4.2 %copy-start = (bf16[256,16]{0,1:T(8,128)(2,1)S(1)}, bf16[256,16]{0,1:T(8,128)(2,1)}, u32[]{:S(2)}) copy-start(bf16[256,16]{0,1:T(8,128)(2,1)} %param.7) | copy-start | bytes 24580
  6.5 73.6 %all-gather.3.cloned.1.call-start = ((), (), s32[]{:S(2)}) async-start(), calls=%async_computation | async-start | bytes 5677056 | tf_op jit(solution)/shard_map/all_gather | solution.py:119
Sparse Core Ops, SparseCore 0:
  11.8 68.2 all-gather.2

commit v3 on v2

--- a/solution.py
+++ b/solution.py
@@ -48,7 +48,90 @@
     per_row = -(-slots // wide)
     rest = jnp.pad(rest, ((0, -rest.shape[0] % 8), (0, per_row * wide - slots)))
     rest = rest.reshape(-1, wide)
+    rest = jnp.pad(rest, ((0, -(slots + rest.shape[0]) % 16), (0, 0)))
     return jnp.concatenate([main, rest], axis=0), wide, per_row, cap
+
+
+def gather_kernel(sky_count, gz_count, block_ref, all_ref, send_sem, recv_sem, own_sem):
+    me, z = lax.axis_index("sky"), lax.axis_index("gz")
+    rows = block_ref.shape[0]
+    cut = (rows // 2 + 15) // 16 * 16
+    bits = [1 << i for i in range(1, sky_count.bit_length() - 1)]
+
+    def flipped(index, p):
+        return index + p * (1 - 2 * ((me // p) % 2))
+
+    barrier = pltpu.get_barrier_semaphore()
+    near = [(me, lax.rem(z + i, gz_count)) for i in range(1, gz_count)]
+    far = [(flipped(me, p), z) for p in [1] + bits]
+    for device in near + far:
+        pl.semaphore_signal(barrier, inc=1, device_id=device, device_id_type=pl.DeviceIdType.MESH)
+    pl.semaphore_wait(barrier, len(near) + len(far))
+
+    started = []
+
+    def send(source, target, device):
+        number = len(started)
+        copy = pltpu.make_async_remote_copy(
+            src_ref=source,
+            dst_ref=target,
+            send_sem=send_sem.at[number],
+            recv_sem=recv_sem.at[number],
+            device_id=device,
+            device_id_type=pl.DeviceIdType.MESH,
+        )
+        copy.start()
+        started.append(copy)
+        return copy
+
+    def piece(group, start, size):
+        return all_ref.at[pl.ds(group * gz_count, gz_count), pl.ds(start, size)]
+
+    mine = all_ref.at[me * gz_count + z]
+    own = pltpu.make_async_copy(block_ref, mine, own_sem)
+    own.start()
+    first = [send(block_ref, mine, device) for device in near]
+    own.wait()
+    for copy in first:
+        copy.wait_recv()
+    across = (flipped(me, 1), z)
+    whole = piece(me, 0, rows)
+    last = [send(whole, whole, across)]
+    halves = [(0, cut, bits), (cut, rows - cut, bits[::-1])]
+    held = [[me], [me]]
+    for step in range(len(bits)):
+        coming = []
+        for h, (start, size, order) in enumerate(halves):
+            device = (flipped(me, order[step]), z)
+            coming.append(
+                [send(piece(g, start, size), piece(g, start, size), device) for g in held[h]]
+            )
+        for h, (start, size, order) in enumerate(halves):
+            new = [flipped(g, order[step]) for g in held[h]]
+            for copy, g in zip(coming[h], new):
+                copy.wait_recv()
+                last.append(send(piece(g, start, size), piece(g, start, size), across))
+            held[h] = held[h] + new
+    for copy in last:
+        copy.wait_recv()
+    for copy in started:
+        copy.wait_send()
+
+
+def gather(block, sky_count, gz_count):
+    copies = gz_count - 1 + 1 + 4 * (sky_count // 2 - 1)
+    return pl.pallas_call(
+        functools.partial(gather_kernel, sky_count, gz_count),
+        out_shape=jax.ShapeDtypeStruct((sky_count * gz_count,) + block.shape, block.dtype),
+        in_specs=[pl.BlockSpec(memory_space=pl.ANY)],
+        out_specs=pl.BlockSpec(memory_space=pl.ANY),
+        scratch_shapes=[
+            pltpu.SemaphoreType.DMA((copies,)),
+            pltpu.SemaphoreType.DMA((copies,)),
+            pltpu.SemaphoreType.DMA,
+        ],
+        compiler_params=pltpu.CompilerParams(collective_id=0, has_side_effects=True),
+    )(block)
 
 
 def cube_kernel(dims, got_ref, tail_ref, wave_ref, spread_ref, turn_ref, out_ref, spec_ref, plane_ref):
@@ -116,8 +199,8 @@
     pad_rows = tile_rows + 8
     block, wide, per_row, cap = pack(spectra, kernel, owner, offset)
     slots = sky_count * cap
-    got = lax.all_gather(block, ("sky", "gz"), axis=0, tiled=False)
-    rest = got[:, slots:].reshape(sky_count, gz_count, -1, per_row * wide)[:, :, :, :slots]
+    got = gather(block, sky_count, gz_count)
+    rest = got[:, slots : slots + (block.shape[0] - slots) // per_row * per_row].reshape(sky_count, gz_count, -1, per_row * wide)[:, :, :, :slots]
     narrow = slab - wide
     taps = KSIDE * KSIDE // gz_count
     tail = rest[:, :, :narrow].reshape(sky_count, gz_count * narrow, slots).transpose(0, 2, 1)

time: 147 us -> 114 us (0.78)
  waiting for transfers between devices: 68.4 us -> 0 us
  Pallas kernels: 49.7 us -> 99 us
  between operations: 13.6 us -> 0.24 us
    all_gather x1 -> x0, waiting for transfers between devices: 68.4 us -> none  [shards(): got = lax.all_gather(block, ('sky', 'gz'), axis=0, tiled=False)]
    pallas_call x0 -> x1, Pallas kernels: none -> 49.4 us  [gather(): pl.pallas_call(functools.partial(gather_kernel, sky_count, gz_count), out...]
  transfers between devices with their start and end apart: 1 -> 0, of which waited for: 1 -> 0; matrix products, arithmetic and copies ran while one was open for 0% -> 0% of each run, Pallas kernels for 0% -> 0%
where the time goes in v3:
time: 114 us
  Pallas kernels  99 us (87%)
  other arithmetic  9.62 us (8%)
  local copies, waits for them, and re-layouts  3.9 us (3%)
  matrix products  1.32 us (1%)
    pallas_call x1, Pallas kernels, shards(): pl.pallas_call(functools.partial(cube_kernel, dims), grid=(chunks,), in_s...  49.7 us
    pallas_call x1, Pallas kernels, gather(): pl.pallas_call(functools.partial(gather_kernel, sky_count, gz_count), out...  49.4 us
    another operation x1, other arithmetic  4.17 us

profile of v3, /device:TPU:9, one launch (start us, length us, event | category | flops | bytes accessed | tf_op | source)
XLA Modules:
  0.0 114.1 jit_solution(11552401099110710503)
XLA Ops:
  0.0 0.0 copy-start
  0.0 0.9 convert_reduce_fusion
  0.9 0.7 multiply_add_fusion.4
  1.6 0.7 slice.75
  2.3 0.7 fusion.32
  3.0 0.0 copy-done
  3.1 0.2 convolution_convert_fusion.1
  3.3 1.1 convolution_convert_fusion
  4.4 0.7 pad_maximum_fusion.4.block_ref
  5.1 49.4 %shard_map.64.got_ref = bf16[32,336,256]{2,1,0:T(8,128)(2,1)} custom-call(bf16[336,256]{1,0:T(8,128)(2,1)} %pad_maximum_fusion.4.block_ref), custom_call_target="tpu_custom_call" | custom-call | tf_op jit(solution)/shard_map/pallas_call | solution.py:123
  54.5 1.0 slice.76
  55.4 0.1 reshape.527
  55.6 0.1 reshape.533
  55.7 0.1 reshape.530
  55.8 0.1 reshape.532
  55.9 0.1 reshape.529
  56.0 0.1 slice.100
  56.1 0.2 reshape.534
  56.3 0.1 copy.25
  56.4 0.2 reshape.531
  56.6 0.2 slice_multiply_fusion.15
  56.9 0.3 fusion.3
  57.2 1.1 copy.19
  58.3 1.6 %fusion.23 = (f32[8,1,8,320]{3,2,1,0:T(8,128)S(1)}, f32[8,1,8,320]{3,2,1,0:T(8,128)S(1)}, f32[8,1,8,320]{3,2,1,0:T(8,128)S(1)}, f32[8,1,8,320]{3,2,1,0:T(8,128)S...) fusion(s32[8,320]{1,0:T(8,128)S(1)} %reshape.530, ...), kind=kLoop, calls=%fused_computation.64 | loop fusion | flops 1228800 | bytes 696352 | tf_op jit(solution)/shard_map/cos | solution.py:223
  59.9 0.1 multiply_add_fusion.2
  60.0 0.1 multiply_add_fusion.1
  60.1 0.1 multiply_add_fusion
  60.2 0.1 multiply_add_fusion.3
  60.3 4.2 %select_convert_fusion = bf16[8,2,8,40,320]{4,3,2,1,0:T(8,128)(2,1)} fusion(bf16[8,2,8,320]{3,2,1,0:T(8,128)(2,1)S(1)} %multiply_add_fusion, bf16[8,2,8,320]{3,2,1,0:T(8,128)(2,1)S(1)} %multiply_add_fusion.1, bf16[8,2,8,320]{3,2,1,0:T(8,128)(2,1)S(1)} %multiply_add_fusion.2, bf16[8,2,8,320]{3,2,1,0:T(8,128)(2,1)S(1)} %multiply_add_fusion.3, ...), kind=kLoop, calls=%fused_computation | loop fusion | flops 6553600 | bytes 4014080 | tf_op jit(solution)/shard_map/convert.9
  64.4 49.7 %shard_map.65 = f32[2,8,1032,256]{3,2,1,0:T(8,128)} custom-call(bf16[32,336,256]{2,1,0:T(8,128)(2,1)} %shard_map.64.got_ref, bf16[8,320,8]{2,1,0:T(8,128)(2,1)} %bitcast.64, bf16[3,1032,768]{2,1,0:T(8,128)(2,1)} %constant.89.clone.wave_ref, bf16[8,640,320]{2,1,0:T(8,128)(2,1)} %bitcast.62, bf16[256,512]{1,0:T(8,128)(2,1)} %constant.90.clone.turn_ref), custom_call_target="tpu_custom_call" | custom-call | flops 24555552768 | bytes 33554432 | tf_op jit(solution)/shard_map/pallas_call | solution.py:250
  (22 shorter events, 0.2 us)
Async XLA Ops:
  0.0 3.0 %copy-start = (bf16[256,16]{0,1:T(8,128)(2,1)S(1)}, bf16[256,16]{0,1:T(8,128)(2,1)}, u32[]{:S(2)}) copy-start(bf16[256,16]{0,1:T(8,128)(2,1)} %param.7) | copy-start | bytes 24580

commit v4 on v3

--- a/solution.py
+++ b/solution.py
@@ -85,33 +85,48 @@
         return copy
 
     def piece(group, start, size):
-        return all_ref.at[pl.ds(group * gz_count, gz_count), pl.ds(start, size)]
+        return all_ref.at[group[0] * gz_count + group[1], pl.ds(start, size)]
 
     mine = all_ref.at[me * gz_count + z]
     own = pltpu.make_async_copy(block_ref, mine, own_sem)
     own.start()
     first = [send(block_ref, mine, device) for device in near]
-    own.wait()
-    for copy in first:
-        copy.wait_recv()
     across = (flipped(me, 1), z)
-    whole = piece(me, 0, rows)
-    last = [send(whole, whole, across)]
     halves = [(0, cut, bits), (cut, rows - cut, bits[::-1])]
-    held = [[me], [me]]
-    for step in range(len(bits)):
-        coming = []
+    lines = [lax.rem(z + gz_count - i, gz_count) for i in range(gz_count)]
+    last = []
+    held = [[[(me, line)], [(me, line)]] for line in lines]
+    coming = [None] * gz_count
+
+    def go_on(i, step):
+        coming[i] = []
         for h, (start, size, order) in enumerate(halves):
             device = (flipped(me, order[step]), z)
-            coming.append(
-                [send(piece(g, start, size), piece(g, start, size), device) for g in held[h]]
+            coming[i].append(
+                [send(piece(g, start, size), piece(g, start, size), device) for g in held[i][h]]
             )
-        for h, (start, size, order) in enumerate(halves):
-            new = [flipped(g, order[step]) for g in held[h]]
-            for copy, g in zip(coming[h], new):
-                copy.wait_recv()
-                last.append(send(piece(g, start, size), piece(g, start, size), across))
-            held[h] = held[h] + new
+
+    for i, line in enumerate(lines):
+        if i == 0:
+            own.wait()
+        else:
+            first[i - 1].wait_recv()
+        go_on(i, 0)
+        whole = piece((me, line), 0, rows)
+        last.append(send(whole, whole, across))
+    for step in range(len(bits)):
+        for i in range(gz_count):
+            arrived = []
+            for h, (start, size, order) in enumerate(halves):
+                new = [(flipped(g, order[step]), line) for g, line in held[i][h]]
+                for copy in coming[i][h]:
+                    copy.wait_recv()
+                held[i][h] = held[i][h] + new
+                arrived += [(g, start, size) for g in new]
+            if step + 1 < len(bits):
+                go_on(i, step + 1)
+            for part in arrived:
+                last.append(send(piece(*part), piece(*part), across))
     for copy in last:
         copy.wait_recv()
     for copy in started:
@@ -119,7 +134,7 @@
 
 
 def gather(block, sky_count, gz_count):
-    copies = gz_count - 1 + 1 + 4 * (sky_count // 2 - 1)
+    copies = gz_count - 1 + gz_count * (1 + 4 * (sky_count // 2 - 1))
     return pl.pallas_call(
         functools.partial(gather_kernel, sky_count, gz_count),
         out_shape=jax.ShapeDtypeStruct((sky_count * gz_count,) + block.shape, block.dtype),

time: 114 us -> 107 us (0.939); the launches traced: 114 us -> 106 us
  Pallas kernels: 99 us -> 90.6 us
    pallas_call x1, Pallas kernels: 49.4 us -> 40.9 us  [gather(): pl.pallas_call(functools.partial(gather_kernel, sky_count, gz_count), out...]
where the time goes in v4:
time: 107 us; the launch traced here: 106 us
  Pallas kernels  90.6 us (85%)
  other arithmetic  9.62 us (9%)
  local copies, waits for them, and re-layouts  3.9 us (4%)
  matrix products  1.32 us (1%)
    pallas_call x1, Pallas kernels, shards(): pl.pallas_call(functools.partial(cube_kernel, dims), grid=(chunks,), in_s...  49.7 us
    pallas_call x1, Pallas kernels, gather(): pl.pallas_call(functools.partial(gather_kernel, sky_count, gz_count), out...  40.9 us
    another operation x1, other arithmetic  4.17 us

profile of v4, /device:TPU:9, one launch (start us, length us, event | category | flops | bytes accessed | tf_op | source)
XLA Modules:
  0.0 105.7 jit_solution(16356288293650660925)
XLA Ops:
  0.0 0.0 copy-start
  0.0 0.9 convert_reduce_fusion
  0.9 0.7 multiply_add_fusion.4
  1.6 0.7 slice.75
  2.3 0.7 fusion.32
  3.0 0.0 copy-done
  3.1 0.2 convolution_convert_fusion.1
  3.3 1.1 %convolution_convert_fusion = bf16[320,256]{1,0:T(8,128)(2,1)S(1)} fusion(s32[256]{0:T(256)S(1)} %multiply_add_fusion.4, bf16[256,258]{0,1:T(8,128)(2,1)} %param.6), kind=kOutput, calls=%fused_computation.1 | convolution fusion | flops 42106880 | bytes 295936 | tf_op jit(solution)/shard_map/dot_general | solution.py:45
  4.4 0.7 pad_maximum_fusion.4.block_ref
  5.1 40.9 %shard_map.64.got_ref = bf16[32,336,256]{2,1,0:T(8,128)(2,1)} custom-call(bf16[336,256]{1,0:T(8,128)(2,1)} %pad_maximum_fusion.4.block_ref), custom_call_target="tpu_custom_call" | custom-call | tf_op jit(solution)/shard_map/pallas_call | solution.py:138
  46.0 1.0 slice.76
  47.0 0.1 reshape.527
  47.2 0.1 reshape.533
  47.3 0.1 reshape.530
  47.3 0.1 reshape.532
  47.4 0.1 reshape.529
  47.6 0.1 slice.100
  47.7 0.2 reshape.534
  47.9 0.1 copy.25
  48.0 0.2 reshape.531
  48.2 0.2 slice_multiply_fusion.15
  48.5 0.3 fusion.3
  48.8 1.1 %copy.19 = bf16[8,8,320]{1,2,0:T(8,128)(2,1)} copy(bf16[8,8,320]{2,0,1:T(8,128)(2,1)S(1)} %bitcast.65) | data formatting | bytes 81920 | tf_op jit(solution)/shard_map/reshape | solution.py:221
  49.9 1.6 %fusion.23 = (f32[8,1,8,320]{3,2,1,0:T(8,128)S(1)}, f32[8,1,8,320]{3,2,1,0:T(8,128)S(1)}, f32[8,1,8,320]{3,2,1,0:T(8,128)S(1)}, f32[8,1,8,320]{3,2,1,0:T(8,128)S...) fusion(s32[8,320]{1,0:T(8,128)S(1)} %reshape.530, ...), kind=kLoop, calls=%fused_computation.64 | loop fusion | flops 1228800 | bytes 696352 | tf_op jit(solution)/shard_map/cos | solution.py:238
  51.5 0.1 multiply_add_fusion.2
  51.6 0.1 multiply_add_fusion.1
  51.7 0.1 multiply_add_fusion
  51.7 0.1 multiply_add_fusion.3
  51.8 4.2 %select_convert_fusion = bf16[8,2,8,40,320]{4,3,2,1,0:T(8,128)(2,1)} fusion(bf16[8,2,8,320]{3,2,1,0:T(8,128)(2,1)S(1)} %multiply_add_fusion, bf16[8,2,8,320]{3,2,1,0:T(8,128)(2,1)S(1)} %multiply_add_fusion.1, bf16[8,2,8,320]{3,2,1,0:T(8,128)(2,1)S(1)} %multiply_add_fusion.2, bf16[8,2,8,320]{3,2,1,0:T(8,128)(2,1)S(1)} %multiply_add_fusion.3, ...), kind=kLoop, calls=%fused_computation | loop fusion | flops 6553600 | bytes 4014080 | tf_op jit(solution)/shard_map/convert.9
  56.0 49.7 %shard_map.65 = f32[2,8,1032,256]{3,2,1,0:T(8,128)} custom-call(bf16[32,336,256]{2,1,0:T(8,128)(2,1)} %shard_map.64.got_ref, bf16[8,320,8]{2,1,0:T(8,128)(2,1)} %bitcast.64, bf16[3,1032,768]{2,1,0:T(8,128)(2,1)} %constant.89.clone.wave_ref, bf16[8,640,320]{2,1,0:T(8,128)(2,1)} %bitcast.62, bf16[256,512]{1,0:T(8,128)(2,1)} %constant.90.clone.turn_ref), custom_call_target="tpu_custom_call" | custom-call | flops 24555552768 | bytes 33554432 | tf_op jit(solution)/shard_map/pallas_call | solution.py:265
  (22 shorter events, 0.2 us)
Async XLA Ops:
  0.0 3.0 %copy-start = (bf16[256,16]{0,1:T(8,128)(2,1)S(1)}, bf16[256,16]{0,1:T(8,128)(2,1)}, u32[]{:S(2)}) copy-start(bf16[256,16]{0,1:T(8,128)(2,1)} %param.7) | copy-start | bytes 24580
